TPU v7x, 32 devices: a whole 2x2x4 slice. The times are simulated.
32 devices in a mesh: groups: 2 (over x), band: 16 (over z, y, core).
Axes of the slice: x: 2, y: 2, z: 4, core: 2. Of those that a mesh axis runs over, the one named last changes fastest.
Arguments:
- tile_blocks: bfloat16 [256, 32, 128, 128], P(('groups', 'band')), parts along dimension 0, may hold values from -0.09375 to 0.09375
- column_ids: int32 [256, 32], P(('groups', 'band')), parts along dimension 0, may hold values from 0 to 383, as said below
- arc_cost: float32 [98304], P(('groups', 'band')), parts along dimension 0, may hold values from 0.25 to 4
- demand_rhs: float32 [32768, 128], P(('groups', 'band')), parts along dimension 0, may hold values from -6 to 6
- primal_start: float32 [98304, 128], P(('groups', 'band')), parts along dimension 0, may hold values from 0.05 to 2
- dual_start: float32 [32768, 128], P(('groups', 'band')), parts along dimension 0, may hold values from -6 to 6
Outputs:
- primal_next: float32 [98304, 128], P(('groups', 'band')), parts along dimension 0
- dual_next: float32 [32768, 128], P(('groups', 'band')), parts along dimension 0
- relative_gap: float32 [256], P('groups'), parts along dimension 0
There are 2 independent parts, one for each index of `groups`. A program takes and returns all parts, laid end to end along the dimension named above; each array names one. Nothing has to cross between parts.
Inputs may be any that keep to these rules, and one draw needn't show every extreme that they name: `column_ids`: row block g lies in band r = g // 8; bands have 24 column blocks each and are counted cyclically. Its 32 column blocks are distinct: the first 6 among the last 8 blocks of band r - 1, the next 20 in band r, the last 6 among the first 8 blocks of band r + 1.
All inputs are finite; a program needn't handle non-finite values.
Results may differ from a plain program's by a relative error of at most 0.0011.
Values may be sent and summed in bfloat16 or wider, within the bound.
A program may use at most 128 MiB of HBM per device.

v0:
```python
import jax
import jax.numpy as jnp
from jax import lax
from jax.sharding import PartitionSpec as P

MB = 8


def extended(block, sides, width):
    for axis, dim in sides:
        count = lax.axis_size(axis)
        forward = [(i, i + 1) for i in range(count - 1)]
        forward.append((count - 1, 0))
        backward = [(target, source) for source, target in forward]
        low = lax.ppermute(
            lax.slice_in_dim(block, block.shape[dim] - width, None, axis=dim), axis, forward
        )
        high = lax.ppermute(lax.slice_in_dim(block, 0, width, axis=dim), axis, backward)
        block = jnp.concatenate([low, block, high], axis=dim)
    return block


def shifted(value, axis, steps):
    count = lax.axis_size(axis)
    pairs = [(source, (source + steps) % count) for source in range(count)]
    return lax.ppermute(value, axis, pairs)


def per_device(tile_blocks, column_ids, arc_cost, demand_rhs, primal_start, dual_start):
    band_count = lax.axis_size("band")
    band_index = lax.axis_index("band")
    row_blocks = tile_blocks.shape[0]
    block_size = tile_blocks.shape[2]
    scen_count = primal_start.shape[1]
    col_blocks = primal_start.shape[0] // block_size
    total_blocks = col_blocks * band_count
    window = col_blocks + 2 * MB
    local_ids = (column_ids - (band_index * col_blocks - MB)) % total_blocks
    cost_sq = jnp.sum(arc_cost * arc_cost)
    rhs_sq = jnp.sum(demand_rhs * demand_rhs, axis=0)
    cost_total, rhs_total = lax.psum((cost_sq, rhs_sq), "band")
    omega = jnp.sqrt(cost_total / (rhs_total + 1e-06))
    tau = 0.3 / omega
    sigma = 0.3 * omega

    def extend(flow_round):
        wide = extended(flow_round, (("band", 0),), MB * block_size)
        return wide.reshape(window, block_size, scen_count)

    def forward(flow_round):
        blocks = extend(flow_round)
        picked = blocks[local_ids]
        result = jnp.einsum(
            "rtij,rtjs->ris", tile_blocks, picked, preferred_element_type=jnp.float32
        )
        return result.reshape(row_blocks * block_size, scen_count)

    dual_mid = dual_start + sigma * (demand_rhs - forward(primal_start.astype(jnp.bfloat16)))
    dual_blocks = dual_mid.astype(jnp.bfloat16).reshape(row_blocks, block_size, scen_count)
    terms = jnp.einsum(
        "rtji,rjs->rtis", tile_blocks, dual_blocks, preferred_element_type=jnp.float32
    )
    summed = jax.ops.segment_sum(
        terms.reshape(-1, block_size, scen_count), local_ids.reshape(-1), num_segments=window
    )
    own_part = summed[MB : MB + col_blocks]
    from_right = shifted(summed[:MB].astype(jnp.bfloat16), "band", -1)
    from_left = shifted(summed[MB + col_blocks :].astype(jnp.bfloat16), "band", 1)
    own_part = own_part.at[col_blocks - MB :].add(from_right.astype(jnp.float32))
    own_part = own_part.at[:MB].add(from_left.astype(jnp.float32))
    adjoint_sum = own_part.reshape(col_blocks * block_size, scen_count)
    primal_next = jnp.maximum(primal_start - tau * (arc_cost[:, None] - adjoint_sum), 0.0)
    primal_obj = jnp.sum(arc_cost[:, None] * primal_next, axis=0)
    extrapolated = (2.0 * primal_next - primal_start).astype(jnp.bfloat16)
    dual_next = dual_mid + sigma * (demand_rhs - forward(extrapolated))
    dual_obj = jnp.sum(demand_rhs * dual_next, axis=0)
    primal_total, dual_total = lax.psum((primal_obj, dual_obj), "band")
    relative_gap = (primal_total - dual_total) / (1.0 + jnp.abs(primal_total) + jnp.abs(dual_total))
    return (primal_next, dual_next, relative_gap)


def solution(mesh):
    in_specs = (
        P(("groups", "band"), None, None, None),
        P(("groups", "band"), None),
        P(("groups", "band")),
        P(("groups", "band"), None),
        P(("groups", "band"), None),
        P(("groups", "band"), None),
    )
    out_specs = (P(("groups", "band"), None), P(("groups", "band"), None), P("groups"))
    return jax.shard_map(
        per_device, mesh=mesh, in_specs=in_specs, out_specs=out_specs, check_vma=False
    )
```

profile of v0, /device:TPU:0, one launch (start us, length us, event | category | flops | bytes accessed | tf_op | source)
XLA Modules:
  0.0 187.0 jit_solution(9892304594840024017)
XLA Ops:
  0.6 0.0 copy-start.7
  0.6 0.0 copy-start.2
  0.7 0.0 copy-start.6
  0.7 1.5 convert_element_type.17
  2.3 0.5 collective-permute-start
  2.8 5.1 %collective-permute-start.1 = (bf16[1024,128]{1,0:T(8,128)(2,1)S(1)}, bf16[1024,128]{1,0:T(8,128)(2,1)S(1)}, u32[]{:S(2)}, u32[]{:S(2)}) collective-permute-start(bf16[1024,128]{1,0:T(8,128)(2,1)S(1)} %get-tuple-element.44), channel_id=1, source_target_pairs={{1,0},{2,1},{3,2},{4,3},{5,4},{6,5},{7,6},{8,7},{9,8},{10,9},{11,1... | collective-permute-start | bytes 786440 | tf_op jit(solution)/shard_map/ppermute | solution.py:18
  7.8 0.0 copy-done.7
  7.8 0.1 reshape.99
  7.9 0.0 copy-done.2
  7.9 0.1 multiply_reduce_fusion.2
  8.1 0.0 copy-done.6
  8.1 0.6 multiply_reduce_fusion.3
  8.7 30.8 %all-reduce.1 = (f32[128]{0:T(128)S(1)}, f32[]{:T(128)}) all-reduce(f32[128]{0:T(128)S(1)} %multiply_reduce_fusion.2, f32[]{:T(128)} %multiply_reduce_fusion.3), channel_id=1, replica_groups=mesh['groups'=2,'band'=16] {'band'}, use_global_device_ids=true, to_apply=%region_3.4 | all-reduce | flops 129 | bytes 1032 | tf_op jit(solution)/shard_map/psum | solution.py:41
  39.4 0.7 broadcast_divide_fusion
  40.1 0.1 reshape.115
  40.2 0.0 collective-permute-done
  40.2 0.0 collective-permute-done.1
  40.2 0.1 pad_maximum_fusion
  40.3 8.6 %gather_fusion = bf16[256,128,128]{2,1,0:T(8,128)(2,1)} fusion(bf16[40,128,128]{2,1,0:T(8,128)(2,1)S(1)} %bitcast.59, s32[1024]{0:T(1024)S(1)} %pad_clamp_fusion), kind=kCustom, calls=%fused_computation | custom fusion | bytes 16778240 | tf_op jit(solution)/shard_map/gather | solution.py:52
  48.9 0.0 slice-start
  48.9 0.0 copy-start.4
  48.9 0.0 slice-start.1
  48.9 8.3 %fusion.16 = f32[8,128,128,1]{1,2,3,0:T(8,128)S(1)} fusion(bf16[8,32,128,128]{3,2,1,0:T(8,128)(2,1)} %param.10, bf16[8,32,128,128]{3,2,1,0:T(8,128)(2,1)} %bitcast.61), kind=kOutput, calls=%fused_computation.37 | convolution fusion | flops 1073741824 | bytes 17301504 | tf_op jit(solution)/shard_map/rtij,rtjs->ris/dot_general | solution.py:53
  57.2 0.0 copy-done.4
  57.2 0.1 fusion.9
  57.3 0.0 slice-done
  57.3 0.0 slice-done.1
  57.3 8.1 %fusion.15 = f32[8,128,32,128]{3,1,2,0:T(8,128)} fusion(bf16[8,128,128,1]{2,1,3,0:T(8,128)(2,1)S(1)} %bitcast.62, bf16[8,32,128,128]{3,2,1,0:T(8,128)(2,1)S(1)} %bitcast.56), kind=kOutput, calls=%fused_computation.36 | convolution fusion | flops 1073741824 | bytes 25427968 | tf_op jit(solution)/shard_map/rtji,rjs->rtis/dot_general | solution.py:60
  65.4 17.4 %copy.11 = f32[256,128,128]{2,1,0:T(8,128)} copy(f32[256,128,128]{1,2,0:T(8,128)} %bitcast.57) | data formatting | bytes 33554432 | tf_op jit(solution)/shard_map/reshape | solution.py:64
  82.8 0.3 broadcast_in_dim.4
  83.1 33.2 %scatter_fusion = f32[40,128,128]{2,1,0:T(8,128)S(1)} fusion(f32[40,128,128]{2,1,0:T(8,128)S(1)} %broadcast_in_dim.4, s32[256]{0:T(256)S(1)} %reshape.115, f32[256,128,128]{2,1,0:T(8,128)} %copy.11), kind=kCustom, calls=%fused_computation.2 | custom fusion | flops 4194304 | bytes 50332672 | tf_op jit(solution)/shard_map/scatter-add | solution.py:63
  116.4 0.2 convert.4
  116.6 0.1 collective-permute-start.2
  116.7 0.0 copy-start
  116.7 0.5 collective-permute-start.3
  117.2 0.1 slice.87
  117.3 3.3 %collective-permute-done.2 = bf16[8,128,128]{2,1,0:T(8,128)(2,1)S(1)} collective-permute-done((bf16[8,128,128]{2,1,0:T(8,128)(2,1)S(1)}, bf16[8,128,128]{2,1,0:T(8,128)(2,1)S(1)}, u32[]{:S(2)}, u32[]{:S(2)}) %collective-permute-start.2) | collective-permute-done | bytes 262176 | tf_op jit(solution)/shard_map/ppermute | solution.py:26
  120.6 4.6 %collective-permute-done.3 = bf16[8,128,128]{2,1,0:T(8,128)(2,1)S(1)} collective-permute-done((bf16[8,128,128]{2,1,0:T(8,128)(2,1)S(1)}, bf16[8,128,128]{2,1,0:T(8,128)(2,1)S(1)}, u32[]{:S(2)}, u32[]{:S(2)}) %collective-permute-start.3) | collective-permute-done | bytes 262176 | tf_op jit(solution)/shard_map/ppermute | solution.py:26
  125.3 0.1 fusion.3
  125.4 0.0 copy-done
  125.4 0.5 multiply_reduce_fusion
  125.9 0.0 copy-start.1
  125.9 0.3 subtract_convert_fusion
  126.2 0.1 collective-permute-start.4
  126.3 4.4 %collective-permute-start.5 = (bf16[1024,128]{1,0:T(8,128)(2,1)S(1)}, bf16[1024,128]{1,0:T(8,128)(2,1)S(1)}, u32[]{:S(2)}, u32[]{:S(2)}) collective-permute-start(bf16[1024,128]{1,0:T(8,128)(2,1)S(1)} %get-tuple-element.42), channel_id=1, source_target_pairs={{1,0},{2,1},{3,2},{4,3},{5,4},{6,5},{7,6},{8,7},{9,8},{10,9},{11,1... | collective-permute-start | bytes 786440 | tf_op jit(solution)/shard_map/ppermute | solution.py:18
  130.7 4.0 %collective-permute-done.4 = bf16[1024,128]{1,0:T(8,128)(2,1)S(1)} collective-permute-done((bf16[1024,128]{1,0:T(8,128)(2,1)S(1)}, bf16[1024,128]{1,0:T(8,128)(2,1)S(1)}, u32[]{:S(2)}, u32[]{:S(2)}) %collective-permute-start.4) | collective-permute-done | bytes 262176 | tf_op jit(solution)/shard_map/ppermute | solution.py:15
  134.8 0.0 collective-permute-done.5
  134.8 0.1 pad_maximum_fusion.1
  134.9 0.0 copy-done.1
  134.9 8.6 %gather_fusion.1 = bf16[256,128,128]{2,1,0:T(8,128)(2,1)} fusion(bf16[40,128,128]{2,1,0:T(8,128)(2,1)S(1)} %bitcast.58, s32[1024]{0:T(1024)S(1)} %pad_clamp_fusion), kind=kCustom, calls=%fused_computation.1 | custom fusion | bytes 16778240 | tf_op jit(solution)/shard_map/gather | solution.py:52
  143.5 0.0 copy-start.3
  143.5 0.0 copy-start.5
  143.5 8.2 %fusion.17 = f32[8,128,128,1]{1,2,3,0:T(8,128)S(1)} fusion(bf16[8,32,128,128]{3,2,1,0:T(8,128)(2,1)} %param.10, bf16[8,32,128,128]{3,2,1,0:T(8,128)(2,1)} %bitcast.60), kind=kOutput, calls=%fused_computation.38 | convolution fusion | flops 1073741824 | bytes 17301504 | tf_op jit(solution)/shard_map/rtij,rtjs->ris/dot_general | solution.py:53
  151.7 0.0 copy-done.3
  151.7 0.0 copy-done.5
  151.7 0.9 multiply_reduce_fusion.1
  152.6 33.9 %all-reduce = (f32[128]{0:T(128)S(1)}, f32[128]{0:T(128)S(1)}) all-reduce(f32[128]{0:T(128)S(1)} %get-tuple-element.33, f32[128]{0:T(128)S(1)} %get-tuple-element.31), channel_id=1, replica_groups=mesh['groups'=2,'band'=16] {'band'}, use_global_device_ids=true, to_apply=%region_8.9 | all-reduce | flops 256 | bytes 2048 | tf_op jit(solution)/shard_map/psum | solution.py:77
  186.5 0.5 add_divide_fusion
  (8 shorter events, 0.2 us)
Async XLA Ops:
  0.6 7.2 %copy-start.7 = (s32[8,32]{1,0:T(8,128)S(1)}, s32[8,32]{1,0:T(8,128)}, u32[]{:S(2)}) copy-start(s32[8,32]{1,0:T(8,128)} %param.11) | copy-start | bytes 3076
  0.6 7.3 %copy-start.2 = (f32[1024,128]{1,0:T(8,128)S(1)}, f32[1024,128]{1,0:T(8,128)}, u32[]{:S(2)}) copy-start(f32[1024,128]{1,0:T(8,128)} %param.13) | copy-start | bytes 1572868
  0.7 7.4 %copy-start.6 = (f32[3072]{0:T(1024)S(1)}, f32[3072]{0:T(1024)}, u32[]{:S(2)}) copy-start(f32[3072]{0:T(1024)} %param.12) | copy-start | bytes 36868
  2.3 37.9 %collective-permute-start = (bf16[1024,128]{1,0:T(8,128)(2,1)S(1)}, bf16[1024,128]{1,0:T(8,128)(2,1)S(1)}, u32[]{:S(2)}, u32[]{:S(2)}) collective-permute-start(bf16[1024,128]{1,0:T(8,128)(2,1)S(1)} %get-tuple-element.43), channel_id=1, source_target_pairs={{0,1},{1,2},{2,3},{3,4},{4,5},{5,6},{6,7},{7,8},{8,9},{9,10},{10,1... | collective-permute-start | bytes 786440 | tf_op jit(solution)/shard_map/ppermute | solution.py:15
  2.8 37.4 %collective-permute-start.1 = (bf16[1024,128]{1,0:T(8,128)(2,1)S(1)}, bf16[1024,128]{1,0:T(8,128)(2,1)S(1)}, u32[]{:S(2)}, u32[]{:S(2)}) collective-permute-start(bf16[1024,128]{1,0:T(8,128)(2,1)S(1)} %get-tuple-element.44), channel_id=1, source_target_pairs={{1,0},{2,1},{3,2},{4,3},{5,4},{6,5},{7,6},{8,7},{9,8},{10,9},{11,1... | collective-permute-start | bytes 786440 | tf_op jit(solution)/shard_map/ppermute | solution.py:18
  48.9 8.4 %slice-start = ((s8[8388608]{0:T(1024)(128)(4,1)}), s8[4194304]{0:T(1024)(128)(4,1)S(1)}, s32[]{:S(2)}) async-start(s8[8388608]{0:T(1024)(128)(4,1)} %bitcast.55), calls=%async_computation | async-start | bytes 8388608
  48.9 8.3 %copy-start.4 = (f32[1024,128]{1,0:T(8,128)S(1)}, f32[1024,128]{1,0:T(8,128)}, u32[]{:S(2)}) copy-start(f32[1024,128]{1,0:T(8,128)} %param.15) | copy-start | bytes 1572868
  48.9 8.4 %slice-start.1 = ((s8[8388608]{0:T(1024)(128)(4,1)}), s8[4194304]{0:T(1024)(128)(4,1)S(1)}, s32[]{:S(2)}) async-start(s8[8388608]{0:T(1024)(128)(4,1)} %bitcast.55), calls=%async_computation.1 | async-start | bytes 8388608
  116.6 3.9 %collective-permute-start.2 = (bf16[8,128,128]{2,1,0:T(8,128)(2,1)S(1)}, bf16[8,128,128]{2,1,0:T(8,128)(2,1)S(1)}, u32[]{:S(2)}, u32[]{:S(2)}) collective-permute-start(bf16[8,128,128]{2,1,0:T(8,128)(2,1)S(1)} %get-tuple-element.40), channel_id=1, source_target_pairs={{0,15},{1,0},{2,1},{3,2},{4,3},{5,4},{6,5},{7,6},{8,7},{9,8},{10,9... | collective-permute-start | bytes 786440 | tf_op jit(solution)/shard_map/ppermute | solution.py:26
  116.7 8.7 %copy-start = (f32[3072,128]{1,0:T(8,128)S(1)}, f32[3072,128]{1,0:T(8,128)}, u32[]{:S(2)}) copy-start(f32[3072,128]{1,0:T(8,128)} %param.14) | copy-start | bytes 4718596
  116.7 8.5 %collective-permute-start.3 = (bf16[8,128,128]{2,1,0:T(8,128)(2,1)S(1)}, bf16[8,128,128]{2,1,0:T(8,128)(2,1)S(1)}, u32[]{:S(2)}, u32[]{:S(2)}) collective-permute-start(bf16[8,128,128]{2,1,0:T(8,128)(2,1)S(1)} %get-tuple-element.39), channel_id=1, source_target_pairs={{0,1},{1,2},{2,3},{3,4},{4,5},{5,6},{6,7},{7,8},{8,9},{9,10},{10,1... | collective-permute-start | bytes 786440 | tf_op jit(solution)/shard_map/ppermute | solution.py:26
  125.9 9.0 %copy-start.1 = (f32[3072,128]{1,0:T(8,128)}, f32[3072,128]{1,0:T(8,128)S(1)}, u32[]{:S(2)}) copy-start(f32[3072,128]{1,0:T(8,128)S(1)} %get-tuple-element.32) | copy-start | bytes 4718596
  126.2 8.5 %collective-permute-start.4 = (bf16[1024,128]{1,0:T(8,128)(2,1)S(1)}, bf16[1024,128]{1,0:T(8,128)(2,1)S(1)}, u32[]{:S(2)}, u32[]{:S(2)}) collective-permute-start(bf16[1024,128]{1,0:T(8,128)(2,1)S(1)} %get-tuple-element.41), channel_id=1, source_target_pairs={{0,1},{1,2},{2,3},{3,4},{4,5},{5,6},{6,7},{7,8},{8,9},{9,10},{10,1... | collective-permute-start | bytes 786440 | tf_op jit(solution)/shard_map/ppermute | solution.py:15
  126.3 8.5 %collective-permute-start.5 = (bf16[1024,128]{1,0:T(8,128)(2,1)S(1)}, bf16[1024,128]{1,0:T(8,128)(2,1)S(1)}, u32[]{:S(2)}, u32[]{:S(2)}) collective-permute-start(bf16[1024,128]{1,0:T(8,128)(2,1)S(1)} %get-tuple-element.42), channel_id=1, source_target_pairs={{1,0},{2,1},{3,2},{4,3},{5,4},{6,5},{7,6},{8,7},{9,8},{10,9},{11,1... | collective-permute-start | bytes 786440 | tf_op jit(solution)/shard_map/ppermute | solution.py:18
  143.5 8.2 %copy-start.3 = (f32[1024,128]{1,0:T(8,128)S(1)}, f32[1024,128]{1,0:T(8,128)}, u32[]{:S(2)}) copy-start(f32[1024,128]{1,0:T(8,128)} %param.13) | copy-start | bytes 1572868
  143.5 8.2 %copy-start.5 = (f32[1024,128]{1,0:T(8,128)S(1)}, f32[1024,128]{1,0:T(8,128)}, u32[]{:S(2)}) copy-start(f32[1024,128]{1,0:T(8,128)} %param.15) | copy-start | bytes 1572868
where the time goes:
time: 188 us; the launch traced here: 187 us
  blocking collectives  64.7 us (34%)
  other arithmetic  39.1 us (21%)
  local copies, waits for them, and re-layouts  35.4 us (19%)
  matrix products  24.5 us (13%)
  waiting for transfers between devices  12 us (6%)
  starting transfers between devices  10.6 us (6%)
    psum x1, blocking collectives, per_device(): primal_total, dual_total = lax.psum((primal_obj, dual_obj), 'band')  33.9 us
    scatter-add x1, other arithmetic, per_device(): jax.ops.segment_sum(terms.reshape(-1, block_size, scen_count), local_ids....  33.2 us
    psum x1, blocking collectives, per_device(): cost_total, rhs_total = lax.psum((cost_sq, rhs_sq), 'band')  30.8 us
    reshape x1, local copies, waits for them, and re-layouts, per_device(): terms.reshape(-1, block_size, scen_count)  17.4 us
    gather x2, local copies, waits for them, and re-layouts, forward(): picked = blocks[local_ids]  17.2 us
    dot_general x2, matrix products, forward(): jnp.einsum('rtij,rtjs->ris', tile_blocks, picked, preferred_element_type=...  16.4 us
    ppermute x2, starting transfers between devices, extended(): lax.ppermute(lax.slice_in_dim(block, 0, width, axis=dim), axis, backward)  9.49 us
    dot_general x1, matrix products, per_device(): jnp.einsum('rtji,rjs->rtis', tile_blocks, dual_blocks, preferred_element_...  8.11 us
  transfers between devices with their start and end apart: 6, of which 3 were waited for; matrix products, arithmetic and copies ran while one was open for 1% of the time, Pallas kernels for 0%

commit v1 on v0

v1 whole, which is shorter than its diff:
```python
import functools

import jax
import jax.numpy as jnp
from jax import lax
from jax.experimental import pallas as pl
from jax.experimental.pallas import tpu as pltpu
from jax.sharding import PartitionSpec as P

MB = 8
BLK = 128
PAIR = 2 * BLK
F32 = jnp.float32
BF16 = jnp.bfloat16
MESH = pl.DeviceIdType.MESH


def kernel(
    n,
    tiles_hbm,
    ids_ref,
    cost_ref,
    rhs_hbm,
    primal_hbm,
    dual_hbm,
    primal_out,
    dual_out,
    gap_out,
    *scratch,
):
    row_blocks, tile_count = ids_ref.shape
    tiles = scratch[:row_blocks]
    (
        dense,
        inv_v,
        inv_s,
        primal,
        cost_col,
        rhs,
        dual,
        acc,
        flow,
        flow2,
        halo_l,
        halo_r,
        halo2_l,
        halo2_r,
        send_l,
        send_r,
        term_l,
        term_r,
        own_adj,
        norm_buf,
        obj_buf,
        tile_sem,
        in_sem,
        inv_sem,
        out_sem,
        halo_send,
        halo_recv,
        norm_send,
        norm_recv,
        obj_send,
        obj_recv,
    ) = scratch[row_blocks:]
    rows = row_blocks * BLK
    ends = MB // 2
    own = primal_hbm.shape[0] // PAIR
    pairs = own + 2 * ends
    col_blocks = 2 * own
    total_blocks = col_blocks * n
    end_rows = ends * PAIR
    mid_rows = (own - 2 * ends) * PAIR

    me = lax.axis_index("band")
    left = lax.rem(me + n - 1, n)
    right = lax.rem(me + 1, n)

    barrier = pltpu.get_barrier_semaphore()

    def greet(k, carry):
        pl.semaphore_signal(
            barrier, inc=1, device_id={"band": lax.rem(me + k, n)}, device_id_type=MESH
        )
        return carry

    lax.fori_loop(1, n, greet, None)

    def load_rows(start, size, k):
        return pltpu.make_async_copy(
            primal_hbm.at[pl.ds(start, size)], primal.at[pl.ds(start, size)], in_sem.at[k]
        )

    head = load_rows(0, end_rows, 0)
    tail = load_rows(end_rows + mid_rows, end_rows, 1)
    middle = load_rows(end_rows, mid_rows, 2)
    rhs_in = pltpu.make_async_copy(rhs_hbm, rhs, in_sem.at[3])
    dual_in = pltpu.make_async_copy(dual_hbm, dual, in_sem.at[4])
    tile_in = [
        pltpu.make_async_copy(
            tiles_hbm.at[g], tiles[g].at[pl.ds(0, tile_count)], tile_sem.at[g]
        )
        for g in range(row_blocks)
    ]
    head.start()
    tail.start()
    rhs_in.start()
    for copy in tile_in[:2]:
        copy.start()
    middle.start()
    for copy in tile_in[2:]:
        copy.start()
    dual_in.start()

    base = me * col_blocks - MB
    local = lax.rem(ids_ref[...] - base + total_blocks, total_blocks)
    lane = lax.broadcasted_iota(jnp.int32, (row_blocks, BLK), 1)
    inverse = jnp.full((row_blocks, BLK), tile_count, jnp.int32)
    for t in range(tile_count):
        inverse = jnp.where(lane == local[:, t : t + 1], t, inverse)
    inv_v[...] = inverse
    inv_copy = pltpu.make_async_copy(inv_v, inv_s, inv_sem)
    inv_copy.start()

    def exchange(kind, side, c, source, target):
        index = (kind * 2 + side) * ends + c
        return pltpu.make_async_remote_copy(
            src_ref=source,
            dst_ref=target,
            send_sem=halo_send.at[index],
            recv_sem=halo_recv.at[index],
            device_id={"band": left if side == 0 else right},
            device_id_type=MESH,
        )

    to_left = [exchange(0, 0, c, flow.at[c], halo_r.at[c]) for c in range(ends)]
    to_right = [
        exchange(0, 1, c, flow.at[own - ends + c], halo_l.at[c]) for c in range(ends)
    ]
    head.wait()
    for c in range(ends):
        flow[c] = primal[c * PAIR : (c + 1) * PAIR].astype(BF16)
    tail.wait()
    for c in range(own - ends, own):
        flow[c] = primal[c * PAIR : (c + 1) * PAIR].astype(BF16)
    pl.semaphore_wait(barrier, n - 1)
    for c in range(ends):
        to_left[c].start()
        to_right[c].start()

    def share(buf, send_sems, recv_sems, k):
        peer = lax.rem(me + k, n)
        return pltpu.make_async_remote_copy(
            src_ref=buf.at[me],
            dst_ref=buf.at[me],
            send_sem=send_sems.at[peer],
            recv_sem=recv_sems.at[me],
            device_id={"band": peer},
            device_id_type=MESH,
        )

    def collect(buf, send_sems, recv_sems, k):
        peer = lax.rem(me + k, n)
        return pltpu.make_async_remote_copy(
            src_ref=buf.at[peer],
            dst_ref=buf.at[peer],
            send_sem=send_sems.at[peer],
            recv_sem=recv_sems.at[peer],
            device_id={"band": peer},
            device_id_type=MESH,
        )

    def share_all(buf, send_sems, recv_sems):
        def step(k, carry):
            share(buf, send_sems, recv_sems, k).start()
            return carry

        lax.fori_loop(1, n, step, None)

    def collect_all(buf, send_sems, recv_sems):
        def step(k, carry):
            copy = collect(buf, send_sems, recv_sems, k)
            copy.wait_recv()
            copy.wait_send()
            return carry

        lax.fori_loop(1, n, step, None)
        return jnp.sum(buf[...], axis=0)

    def stack(first, second):
        return jnp.concatenate([first, second, jnp.zeros((6, BLK), F32)], axis=0)

    rhs_in.wait()
    rhs_sq = jnp.sum(rhs[...] * rhs[...], axis=0, keepdims=True)
    cost_sq = jnp.sum(cost_ref[...] * cost_ref[...], axis=0, keepdims=True)
    norm_buf[me] = stack(rhs_sq, cost_sq)
    share_all(norm_buf, norm_send, norm_recv)

    for w in range(col_blocks):
        cost_col[w * BLK : (w + 1) * BLK] = jnp.transpose(
            jnp.broadcast_to(cost_ref[w : w + 1, :], (BLK, BLK))
        )
    middle.wait()
    for c in range(ends, own - ends):
        flow[c] = primal[c * PAIR : (c + 1) * PAIR].astype(BF16)

    inv_copy.wait()
    for g in range(row_blocks):
        tiles[g][tile_count] = jnp.zeros((BLK, BLK), BF16)
        tile_in[g].wait()

        def place(p, carry, g=g):
            for half in range(2):
                dense[p, g * BLK : (g + 1) * BLK, half * BLK : (half + 1) * BLK] = tiles[g][
                    inv_s[g, 2 * p + half]
                ]
            return carry

        lax.fori_loop(0, pairs, place, None, unroll=4)

    def product(p, block):
        return jnp.dot(dense[p], block, preferred_element_type=F32)

    acc[...] = product(ends, flow[0])

    def own_step(p, carry):
        acc[...] += product(ends + p, flow[p])
        return carry

    lax.fori_loop(1, own, own_step, None)
    for c in range(ends):
        to_right[c].wait_recv()
        acc[...] += product(c, halo_l[c])
        to_left[c].wait_recv()
        acc[...] += product(ends + own + c, halo_r[c])

    norms = collect_all(norm_buf, norm_send, norm_recv)
    cost_total = jnp.sum(norms[1:2], axis=1, keepdims=True)
    omega = jnp.sqrt(cost_total / (norms[0:1] + 1e-06))
    tau = 0.3 / omega
    sigma = 0.3 * omega

    dual_in.wait()
    dual_mid = dual[...] + sigma * (rhs[...] - acc[...])
    dual[...] = dual_mid
    dual_t = jnp.transpose(dual_mid).astype(BF16)

    def adjoint(p):
        flat = jnp.dot(dual_t, dense[p], preferred_element_type=F32)
        return jnp.transpose(flat)

    terms_left = [exchange(1, 0, c, send_l.at[c], term_r.at[c]) for c in range(ends)]
    terms_right = [exchange(1, 1, c, send_r.at[c], term_l.at[c]) for c in range(ends)]
    for c in range(ends):
        send_l[c] = adjoint(c).astype(BF16)
        terms_left[c].start()
        send_r[c] = adjoint(ends + own + c).astype(BF16)
        terms_right[c].start()

    for c in range(ends):
        own_adj[c] = adjoint(ends + c)
        own_adj[ends + c] = adjoint(own + c)

    def advance(p, total):
        span = slice(p * PAIR, (p + 1) * PAIR)
        start = primal[span]
        cost = cost_col[span]
        following = jnp.maximum(start - tau * (cost - total), 0.0)
        flow2[p] = (2.0 * following - start).astype(BF16)
        primal[span] = following
        store = pltpu.make_async_copy(
            primal.at[pl.ds(p * PAIR, PAIR)],
            primal_out.at[pl.ds(p * PAIR, PAIR)],
            out_sem.at[p],
        )
        store.start()
        return store, jnp.sum(cost * following, axis=0, keepdims=True)

    stores = []
    primal_obj = jnp.zeros((1, BLK), F32)
    for p in range(ends, own - ends):
        store, part = advance(p, adjoint(ends + p))
        stores.append(store)
        primal_obj += part
    acc[...] = product(2 * ends, flow2[ends])
    for p in range(ends + 1, own - ends):
        acc[...] += product(ends + p, flow2[p])

    flow_left = [exchange(2, 0, c, flow2.at[c], halo2_r.at[c]) for c in range(ends)]
    flow_right = [
        exchange(2, 1, c, flow2.at[own - ends + c], halo2_l.at[c]) for c in range(ends)
    ]
    for c in range(ends):
        terms_right[c].wait_recv()
        store, part = advance(c, own_adj[c] + term_l[c].astype(F32))
        stores.append(store)
        primal_obj += part
        flow_left[c].start()
        terms_left[c].wait_recv()
        store, part = advance(own - ends + c, own_adj[ends + c] + term_r[c].astype(F32))
        stores.append(store)
        primal_obj += part
        flow_right[c].start()
    for c in range(ends):
        acc[...] += product(ends + c, flow2[c])
        acc[...] += product(own + c, flow2[own - ends + c])
    for c in range(ends):
        flow_right[c].wait_recv()
        acc[...] += product(c, halo2_l[c])
        flow_left[c].wait_recv()
        acc[...] += product(ends + own + c, halo2_r[c])

    dual_next = dual[...] + sigma * (rhs[...] - acc[...])
    acc[...] = dual_next
    dual_store = pltpu.make_async_copy(acc, dual_out, in_sem.at[5])
    dual_store.start()
    dual_obj = jnp.sum(rhs[...] * dual_next, axis=0, keepdims=True)
    obj_buf[me] = stack(primal_obj, dual_obj)
    share_all(obj_buf, obj_send, obj_recv)
    for copy in to_left + to_right + terms_left + terms_right + flow_left + flow_right:
        copy.wait_send()
    for store in stores:
        store.wait()
    totals = collect_all(obj_buf, obj_send, obj_recv)
    primal_total = totals[0:1]
    dual_total = totals[1:2]
    gap_out[...] = (primal_total - dual_total) / (
        1.0 + jnp.abs(primal_total) + jnp.abs(dual_total)
    )
    dual_store.wait()


def per_device(n, tile_blocks, column_ids, arc_cost, demand_rhs, primal_start, dual_start):
    row_blocks, tile_count = column_ids.shape
    cols, scen = primal_start.shape
    rows = demand_rhs.shape[0]
    own = cols // PAIR
    ends = MB // 2
    pairs = own + 2 * ends
    any_space = pl.BlockSpec(memory_space=pl.ANY)
    vmem = pl.BlockSpec(memory_space=pltpu.VMEM)
    halo = pltpu.VMEM((ends, PAIR, scen), BF16)
    dma = pltpu.SemaphoreType.DMA
    scratch = [pltpu.VMEM((tile_count + 1, BLK, BLK), BF16) for _ in range(row_blocks)]
    scratch += [
        pltpu.VMEM((pairs, rows, PAIR), BF16),
        pltpu.VMEM((row_blocks, BLK), jnp.int32),
        pltpu.SMEM((row_blocks, BLK), jnp.int32),
        pltpu.VMEM((cols, scen), F32),
        pltpu.VMEM((cols, scen), F32),
        pltpu.VMEM((rows, scen), F32),
        pltpu.VMEM((rows, scen), F32),
        pltpu.VMEM((rows, scen), F32),
        pltpu.VMEM((own, PAIR, scen), BF16),
        pltpu.VMEM((own, PAIR, scen), BF16),
        halo,
        halo,
        halo,
        halo,
        halo,
        halo,
        halo,
        halo,
        pltpu.VMEM((2 * ends, PAIR, scen), F32),
        pltpu.VMEM((n, 8, scen), F32),
        pltpu.VMEM((n, 8, scen), F32),
        dma((row_blocks,)),
        dma((6,)),
        dma,
        dma((own,)),
        dma((6 * ends,)),
        dma((6 * ends,)),
        dma((n,)),
        dma((n,)),
        dma((n,)),
        dma((n,)),
    ]
    flops = 3 * 2 * pairs * PAIR * rows * scen
    primal_next, dual_next, gap = pl.pallas_call(
        functools.partial(kernel, n),
        out_shape=(
            jax.ShapeDtypeStruct((cols, scen), F32),
            jax.ShapeDtypeStruct((rows, scen), F32),
            jax.ShapeDtypeStruct((1, scen), F32),
        ),
        in_specs=[any_space, vmem, vmem, any_space, any_space, any_space],
        out_specs=(any_space, any_space, vmem),
        scratch_shapes=scratch,
        compiler_params=pltpu.CompilerParams(
            collective_id=0, has_side_effects=True, vmem_limit_bytes=48 * 1024 * 1024
        ),
        cost_estimate=pl.CostEstimate(
            flops=flops, bytes_accessed=2 * tile_blocks.size + 8 * cols * scen, transcendentals=0
        ),
    )(
        tile_blocks,
        column_ids,
        arc_cost.reshape(cols // BLK, BLK),
        demand_rhs,
        primal_start,
        dual_start,
    )
    return primal_next, dual_next, gap.reshape(scen)


def solution(mesh):
    in_specs = (
        P(("groups", "band"), None, None, None),
        P(("groups", "band"), None),
        P(("groups", "band")),
        P(("groups", "band"), None),
        P(("groups", "band"), None),
        P(("groups", "band"), None),
    )
    out_specs = (P(("groups", "band"), None), P(("groups", "band"), None), P("groups"))
    return jax.shard_map(
        functools.partial(per_device, mesh.shape["band"]),
        mesh=mesh,
        in_specs=in_specs,
        out_specs=out_specs,
        check_vma=False,
    )
```

time: 188 us -> 44 us (0.23)
  blocking collectives: 64.7 us -> 0 us
  other arithmetic: 39.1 us -> 0 us
  Pallas kernels: 0 us -> 35.7 us
  local copies, waits for them, and re-layouts: 35.4 us -> 7.32 us
  matrix products: 24.5 us -> 0 us
  waiting for transfers between devices: 12 us -> 0 us
  starting transfers between devices: 10.6 us -> 0 us
    psum x2 -> x0, blocking collectives: 64.7 us -> none  [the longest x1 33.9 us: per_device(): primal_total, dual_total = lax.psum((primal_obj, dual_obj), 'band')]
    pallas_call x0 -> x1, Pallas kernels: none -> 35.7 us  [per_device(): pl.pallas_call(functools.partial(kernel, n), out_shape=(jax.ShapeDtypeStr...]
    scatter-add x3 -> x0, other arithmetic: 33.4 us -> none  [the longest x1 33.2 us: per_device(): jax.ops.segment_sum(terms.reshape(-1, block_size, scen_count), local_ids....]
    dot_general x3 -> x0, matrix products: 24.5 us -> none  [the longest x2 16.4 us: forward(): jnp.einsum('rtij,rtjs->ris', tile_blocks, picked, preferred_element_type=...]
    reshape x1 -> x0, local copies, waits for them, and re-layouts: 17.4 us -> none  [per_device(): terms.reshape(-1, block_size, scen_count)]
    gather x2 -> x0, local copies, waits for them, and re-layouts: 17.2 us -> none  [forward(): picked = blocks[local_ids]]
    ppermute x6 -> x0, waiting for transfers between devices: 12 us -> none  [the longest x2 7.89 us: shifted(): return lax.ppermute(value, axis, pairs)]
    ppermute x6 -> x0, starting transfers between devices: 10.6 us -> none  [the longest x2 9.49 us: extended(): lax.ppermute(lax.slice_in_dim(block, 0, width, axis=dim), axis, backward)]
  transfers between devices with their start and end apart: 6 -> 0, of which waited for: 3 -> 0; matrix products, arithmetic and copies ran while one was open for 1% -> 0% of each run, Pallas kernels for 0% -> 0%
where the time goes in v1:
time: 44 us; the launch traced here: 43.7 us
  Pallas kernels  35.7 us (81%)
  local copies, waits for them, and re-layouts  7.32 us (17%)
  between operations  0.65 us (1%)
    pallas_call x1, Pallas kernels, per_device(): pl.pallas_call(functools.partial(kernel, n), out_shape=(jax.ShapeDtypeStr...  35.7 us
    unnamed x13, local copies, waits for them, and re-layouts  7.32 us

profile of v1, /device:TPU:0, one launch (start us, length us, event | category | flops | bytes accessed | tf_op | source)
XLA Modules:
  0.0 43.7 jit_solution(4797806504564542118)
XLA Ops:
  0.6 0.0 copy-start
  0.6 1.4 %copy-done = f32[3072,128]{1,0:T(8,128)S(1)} copy-done((f32[3072,128]{1,0:T(8,128)S(1)}, f32[3072,128]{1,0:T(8,128)}, u32[]{:S(2)}) %copy-start) | copy-done | bytes 1572888
  2.0 0.0 copy-start.1
  2.0 1.0 %copy-done.1 = f32[1024,128]{1,0:T(8,128)S(1)} copy-done((f32[1024,128]{1,0:T(8,128)S(1)}, f32[1024,128]{1,0:T(8,128)}, u32[]{:S(2)}) %copy-start.1) | copy-done | bytes 524312
  3.1 0.0 copy-start.2
  3.1 1.0 %copy-done.2 = f32[1024,128]{1,0:T(8,128)S(1)} copy-done((f32[1024,128]{1,0:T(8,128)S(1)}, f32[1024,128]{1,0:T(8,128)}, u32[]{:S(2)}) %copy-start.2) | copy-done | bytes 524312
  4.1 0.0 copy-start.3
  4.1 0.7 %copy-done.3 = f32[3072]{0:T(1024)S(1)} copy-done((f32[3072]{0:T(1024)S(1)}, f32[3072]{0:T(1024)}, u32[]{:S(2)}) %copy-start.3) | copy-done | bytes 12312
  4.8 0.0 copy-start.4
  4.8 0.7 %copy-done.4 = s32[8,32]{1,0:T(8,128)S(1)} copy-done((s32[8,32]{1,0:T(8,128)S(1)}, s32[8,32]{1,0:T(8,128)}, u32[]{:S(2)}) %copy-start.4) | copy-done | bytes 1048
  5.5 35.7 %shard_map.85 = (f32[3072,128]{1,0:T(8,128)S(1)}, f32[1024,128]{1,0:T(8,128)S(1)}, f32[1,128]{1,0:T(1,128)S(1)}) custom-call(bf16[8,32,128,128]{3,2,1,0:T(8,128)(2,1)} %tiles_hbm.1, s32[8,32]{1,0:T(8,128)S(1)} %copy-done.4, f32[24,128]{1,0:T(8,128)S(1)} %bitcast.2, f32[1024,128]{1,0:T(8,128)S(1)} %copy-done.1, f32[3072,128]{1,0:T(8,128)S(1)} %copy-done, ...), custom_call_target="tpu_custom_call" | custom-call | flops 4026531840 | bytes 11534336 | tf_op jit(solution)/shard_map/pallas_call | solution.py:379
  41.3 1.1 %copy.12 = f32[3072,128]{1,0:T(8,128)} copy(f32[3072,128]{1,0:T(8,128)S(1)} %get-tuple-element.12) | data formatting | bytes 3145728
  42.4 0.8 %copy.13 = f32[1024,128]{1,0:T(8,128)} copy(f32[1024,128]{1,0:T(8,128)S(1)} %get-tuple-element.13) | data formatting | bytes 1048576
  43.2 0.5 %copy.14 = f32[128]{0:T(128)} copy(f32[128]{0:T(128)S(1)} %bitcast.3) | data formatting | bytes 1024
Async XLA Ops:
  0.6 1.4 %copy-start = (f32[3072,128]{1,0:T(8,128)S(1)}, f32[3072,128]{1,0:T(8,128)}, u32[]{:S(2)}) copy-start(f32[3072,128]{1,0:T(8,128)} %primal_hbm.1) | copy-start | bytes 4718596
  2.0 1.0 %copy-start.1 = (f32[1024,128]{1,0:T(8,128)S(1)}, f32[1024,128]{1,0:T(8,128)}, u32[]{:S(2)}) copy-start(f32[1024,128]{1,0:T(8,128)} %rhs_hbm.1) | copy-start | bytes 1572868
  3.1 1.0 %copy-start.2 = (f32[1024,128]{1,0:T(8,128)S(1)}, f32[1024,128]{1,0:T(8,128)}, u32[]{:S(2)}) copy-start(f32[1024,128]{1,0:T(8,128)} %dual_hbm.1) | copy-start | bytes 1572868
  4.1 0.7 %copy-start.3 = (f32[3072]{0:T(1024)S(1)}, f32[3072]{0:T(1024)}, u32[]{:S(2)}) copy-start(f32[3072]{0:T(1024)} %param.8) | copy-start | bytes 36868
  4.8 0.7 %copy-start.4 = (s32[8,32]{1,0:T(8,128)S(1)}, s32[8,32]{1,0:T(8,128)}, u32[]{:S(2)}) copy-start(s32[8,32]{1,0:T(8,128)} %ids_ref.1) | copy-start | bytes 3076

commit v2 on v1

--- a/solution.py
+++ b/solution.py
@@ -25,7 +25,7 @@
     dual_hbm,
     primal_out,
     dual_out,
-    gap_out,
+    totals_out,
     *scratch,
 ):
     row_blocks, tile_count = ids_ref.shape
@@ -55,7 +55,6 @@
         tile_sem,
         in_sem,
         inv_sem,
-        out_sem,
         halo_send,
         halo_recv,
         norm_send,
@@ -122,6 +121,9 @@
     inv_copy = pltpu.make_async_copy(inv_v, inv_s, inv_sem)
     inv_copy.start()
 
+    def chunk(ref, c):
+        return ref.at[pl.ds(c * PAIR, PAIR)]
+
     def exchange(kind, side, c, source, target):
         index = (kind * 2 + side) * ends + c
         return pltpu.make_async_remote_copy(
@@ -133,16 +135,16 @@
             device_id_type=MESH,
         )
 
-    to_left = [exchange(0, 0, c, flow.at[c], halo_r.at[c]) for c in range(ends)]
+    to_left = [exchange(0, 0, c, chunk(flow, c), chunk(halo_r, c)) for c in range(ends)]
     to_right = [
-        exchange(0, 1, c, flow.at[own - ends + c], halo_l.at[c]) for c in range(ends)
+        exchange(0, 1, c, chunk(flow, own - ends + c), chunk(halo_l, c)) for c in range(ends)
     ]
     head.wait()
     for c in range(ends):
-        flow[c] = primal[c * PAIR : (c + 1) * PAIR].astype(BF16)
+        flow[c * PAIR : (c + 1) * PAIR] = primal[c * PAIR : (c + 1) * PAIR].astype(BF16)
     tail.wait()
     for c in range(own - ends, own):
-        flow[c] = primal[c * PAIR : (c + 1) * PAIR].astype(BF16)
+        flow[c * PAIR : (c + 1) * PAIR] = primal[c * PAIR : (c + 1) * PAIR].astype(BF16)
     pl.semaphore_wait(barrier, n - 1)
     for c in range(ends):
         to_left[c].start()
@@ -202,7 +204,7 @@
         )
     middle.wait()
     for c in range(ends, own - ends):
-        flow[c] = primal[c * PAIR : (c + 1) * PAIR].astype(BF16)
+        flow[c * PAIR : (c + 1) * PAIR] = primal[c * PAIR : (c + 1) * PAIR].astype(BF16)
 
     inv_copy.wait()
     for g in range(row_blocks):
@@ -211,28 +213,51 @@
 
         def place(p, carry, g=g):
             for half in range(2):
-                dense[p, g * BLK : (g + 1) * BLK, half * BLK : (half + 1) * BLK] = tiles[g][
+                start = pl.multiple_of((2 * p + half) * BLK, BLK)
+                dense[g * BLK : (g + 1) * BLK, pl.ds(start, BLK)] = tiles[g][
                     inv_s[g, 2 * p + half]
                 ]
             return carry
 
         lax.fori_loop(0, pairs, place, None, unroll=4)
 
-    def product(p, block):
-        return jnp.dot(dense[p], block, preferred_element_type=F32)
-
-    acc[...] = product(ends, flow[0])
-
-    def own_step(p, carry):
-        acc[...] += product(ends + p, flow[p])
-        return carry
-
-    lax.fori_loop(1, own, own_step, None)
-    for c in range(ends):
-        to_right[c].wait_recv()
-        acc[...] += product(c, halo_l[c])
-        to_left[c].wait_recv()
-        acc[...] += product(ends + own + c, halo_r[c])
+    left_end = end_rows
+    right_end = (ends + own) * PAIR
+    part_rows = 2 * BLK
+
+    def product(start, block, first=False):
+        size = block.shape[0]
+
+        def step(i, carry):
+            at = pl.ds(pl.multiple_of(i * part_rows, part_rows), part_rows)
+            value = jnp.dot(
+                dense[at, start : start + size], block[...], preferred_element_type=F32
+            )
+            acc[at] = value if first else acc[at] + value
+            return carry
+
+        lax.fori_loop(0, rows // part_rows, step, None)
+
+    def halo_products(low, low_copies, high, high_copies):
+        half = ends // 2
+        for h in range(2):
+            for c in range(h * half, (h + 1) * half):
+                low_copies[c].wait_recv()
+                high_copies[c].wait_recv()
+            at = h * half * PAIR
+            for i in range(0, rows, part_rows):
+                acc[i : i + part_rows] += jnp.dot(
+                    dense[i : i + part_rows, at : at + half * PAIR],
+                    low[at : at + half * PAIR],
+                    preferred_element_type=F32,
+                ) + jnp.dot(
+                    dense[i : i + part_rows, right_end + at : right_end + at + half * PAIR],
+                    high[at : at + half * PAIR],
+                    preferred_element_type=F32,
+                )
+
+    product(left_end, flow, True)
+    halo_products(halo_l, to_right, halo_r, to_left)
 
     norms = collect_all(norm_buf, norm_send, norm_recv)
     cost_total = jnp.sum(norms[1:2], axis=1, keepdims=True)
@@ -246,15 +271,17 @@
     dual_t = jnp.transpose(dual_mid).astype(BF16)
 
     def adjoint(p):
-        flat = jnp.dot(dual_t, dense[p], preferred_element_type=F32)
+        flat = jnp.dot(
+            dual_t, dense[:, p * PAIR : (p + 1) * PAIR], preferred_element_type=F32
+        )
         return jnp.transpose(flat)
 
-    terms_left = [exchange(1, 0, c, send_l.at[c], term_r.at[c]) for c in range(ends)]
-    terms_right = [exchange(1, 1, c, send_r.at[c], term_l.at[c]) for c in range(ends)]
+    terms_left = [exchange(1, 0, c, chunk(send_l, c), chunk(term_r, c)) for c in range(ends)]
+    terms_right = [exchange(1, 1, c, chunk(send_r, c), chunk(term_l, c)) for c in range(ends)]
     for c in range(ends):
-        send_l[c] = adjoint(c).astype(BF16)
+        send_l[c * PAIR : (c + 1) * PAIR] = adjoint(c).astype(BF16)
         terms_left[c].start()
-        send_r[c] = adjoint(ends + own + c).astype(BF16)
+        send_r[c * PAIR : (c + 1) * PAIR] = adjoint(ends + own + c).astype(BF16)
         terms_right[c].start()
 
     for c in range(ends):
@@ -266,68 +293,52 @@
         start = primal[span]
         cost = cost_col[span]
         following = jnp.maximum(start - tau * (cost - total), 0.0)
-        flow2[p] = (2.0 * following - start).astype(BF16)
-        primal[span] = following
-        store = pltpu.make_async_copy(
-            primal.at[pl.ds(p * PAIR, PAIR)],
-            primal_out.at[pl.ds(p * PAIR, PAIR)],
-            out_sem.at[p],
-        )
-        store.start()
-        return store, jnp.sum(cost * following, axis=0, keepdims=True)
-
-    stores = []
+        flow2[span] = (2.0 * following - start).astype(BF16)
+        primal_out[span] = following
+        return jnp.sum(cost * following, axis=0, keepdims=True)
+
     primal_obj = jnp.zeros((1, BLK), F32)
     for p in range(ends, own - ends):
-        store, part = advance(p, adjoint(ends + p))
-        stores.append(store)
-        primal_obj += part
-    acc[...] = product(2 * ends, flow2[ends])
-    for p in range(ends + 1, own - ends):
-        acc[...] += product(ends + p, flow2[p])
-
-    flow_left = [exchange(2, 0, c, flow2.at[c], halo2_r.at[c]) for c in range(ends)]
+        primal_obj += advance(p, adjoint(ends + p))
+    product(left_end + end_rows, flow2.at[pl.ds(end_rows, mid_rows)], True)
+
+    flow_left = [exchange(2, 0, c, chunk(flow2, c), chunk(halo2_r, c)) for c in range(ends)]
     flow_right = [
-        exchange(2, 1, c, flow2.at[own - ends + c], halo2_l.at[c]) for c in range(ends)
+        exchange(2, 1, c, chunk(flow2, own - ends + c), chunk(halo2_l, c)) for c in range(ends)
     ]
     for c in range(ends):
         terms_right[c].wait_recv()
-        store, part = advance(c, own_adj[c] + term_l[c].astype(F32))
-        stores.append(store)
-        primal_obj += part
+        primal_obj += advance(c, own_adj[c] + term_l[c * PAIR : (c + 1) * PAIR].astype(F32))
         flow_left[c].start()
         terms_left[c].wait_recv()
-        store, part = advance(own - ends + c, own_adj[ends + c] + term_r[c].astype(F32))
-        stores.append(store)
-        primal_obj += part
+        primal_obj += advance(own - ends + c, own_adj[ends + c] + term_r[c * PAIR : (c + 1) * PAIR].astype(F32))
         flow_right[c].start()
-    for c in range(ends):
-        acc[...] += product(ends + c, flow2[c])
-        acc[...] += product(own + c, flow2[own - ends + c])
-    for c in range(ends):
-        flow_right[c].wait_recv()
-        acc[...] += product(c, halo2_l[c])
-        flow_left[c].wait_recv()
-        acc[...] += product(ends + own + c, halo2_r[c])
+    product(left_end, flow2.at[pl.ds(0, end_rows)])
+    product(right_end - end_rows, flow2.at[pl.ds(end_rows + mid_rows, end_rows)])
+    halo_products(halo2_l, flow_right, halo2_r, flow_left)
 
     dual_next = dual[...] + sigma * (rhs[...] - acc[...])
-    acc[...] = dual_next
-    dual_store = pltpu.make_async_copy(acc, dual_out, in_sem.at[5])
-    dual_store.start()
+    dual_out[...] = dual_next
     dual_obj = jnp.sum(rhs[...] * dual_next, axis=0, keepdims=True)
     obj_buf[me] = stack(primal_obj, dual_obj)
     share_all(obj_buf, obj_send, obj_recv)
     for copy in to_left + to_right + terms_left + terms_right + flow_left + flow_right:
         copy.wait_send()
-    for store in stores:
-        store.wait()
-    totals = collect_all(obj_buf, obj_send, obj_recv)
+    totals_out[...] = collect_all(obj_buf, obj_send, obj_recv)
+
+
+def finish(primal_in, dual_in, totals, primal_out, dual_out, gap_out, sems):
+    first = pltpu.make_async_copy(primal_in, primal_out, sems.at[0])
+    second = pltpu.make_async_copy(dual_in, dual_out, sems.at[1])
+    first.start()
+    second.start()
     primal_total = totals[0:1]
     dual_total = totals[1:2]
     gap_out[...] = (primal_total - dual_total) / (
         1.0 + jnp.abs(primal_total) + jnp.abs(dual_total)
     )
-    dual_store.wait()
+    first.wait()
+    second.wait()
 
 
 def per_device(n, tile_blocks, column_ids, arc_cost, demand_rhs, primal_start, dual_start):
@@ -338,12 +349,13 @@
     ends = MB // 2
     pairs = own + 2 * ends
     any_space = pl.BlockSpec(memory_space=pl.ANY)
+    hbm = pl.BlockSpec(memory_space=pltpu.HBM)
     vmem = pl.BlockSpec(memory_space=pltpu.VMEM)
-    halo = pltpu.VMEM((ends, PAIR, scen), BF16)
+    halo = pltpu.VMEM((ends * PAIR, scen), BF16)
     dma = pltpu.SemaphoreType.DMA
     scratch = [pltpu.VMEM((tile_count + 1, BLK, BLK), BF16) for _ in range(row_blocks)]
     scratch += [
-        pltpu.VMEM((pairs, rows, PAIR), BF16),
+        pltpu.VMEM((rows, pairs * PAIR), BF16),
         pltpu.VMEM((row_blocks, BLK), jnp.int32),
         pltpu.SMEM((row_blocks, BLK), jnp.int32),
         pltpu.VMEM((cols, scen), F32),
@@ -351,8 +363,8 @@
         pltpu.VMEM((rows, scen), F32),
         pltpu.VMEM((rows, scen), F32),
         pltpu.VMEM((rows, scen), F32),
-        pltpu.VMEM((own, PAIR, scen), BF16),
-        pltpu.VMEM((own, PAIR, scen), BF16),
+        pltpu.VMEM((cols, scen), BF16),
+        pltpu.VMEM((cols, scen), BF16),
         halo,
         halo,
         halo,
@@ -365,9 +377,8 @@
         pltpu.VMEM((n, 8, scen), F32),
         pltpu.VMEM((n, 8, scen), F32),
         dma((row_blocks,)),
-        dma((6,)),
+        dma((5,)),
         dma,
-        dma((own,)),
         dma((6 * ends,)),
         dma((6 * ends,)),
         dma((n,)),
@@ -376,18 +387,18 @@
         dma((n,)),
     ]
     flops = 3 * 2 * pairs * PAIR * rows * scen
-    primal_next, dual_next, gap = pl.pallas_call(
+    outs = pl.pallas_call(
         functools.partial(kernel, n),
         out_shape=(
-            jax.ShapeDtypeStruct((cols, scen), F32),
-            jax.ShapeDtypeStruct((rows, scen), F32),
-            jax.ShapeDtypeStruct((1, scen), F32),
+            pltpu.VMEM((cols, scen), F32),
+            pltpu.VMEM((rows, scen), F32),
+            pltpu.VMEM((8, scen), F32),
         ),
-        in_specs=[any_space, vmem, vmem, any_space, any_space, any_space],
-        out_specs=(any_space, any_space, vmem),
+        in_specs=[hbm, vmem, vmem, hbm, hbm, hbm],
+        out_specs=(vmem, vmem, vmem),
         scratch_shapes=scratch,
         compiler_params=pltpu.CompilerParams(
-            collective_id=0, has_side_effects=True, vmem_limit_bytes=48 * 1024 * 1024
+            collective_id=0, has_side_effects=True, vmem_limit_bytes=56 * 1024 * 1024
         ),
         cost_estimate=pl.CostEstimate(
             flops=flops, bytes_accessed=2 * tile_blocks.size + 8 * cols * scen, transcendentals=0
@@ -400,6 +411,18 @@
         primal_start,
         dual_start,
     )
+    primal_next, dual_next, gap = pl.pallas_call(
+        finish,
+        out_shape=(
+            jax.ShapeDtypeStruct((cols, scen), F32),
+            jax.ShapeDtypeStruct((rows, scen), F32),
+            jax.ShapeDtypeStruct((1, scen), F32),
+        ),
+        in_specs=[any_space, any_space, vmem],
+        out_specs=(hbm, hbm, vmem),
+        scratch_shapes=[dma((2,))],
+        compiler_params=pltpu.CompilerParams(vmem_limit_bytes=1024 * 1024),
+    )(*outs)
     return primal_next, dual_next, gap.reshape(scen)
 
 

time: 44 us -> 38 us (0.86)
  local copies, waits for them, and re-layouts: 7.32 us -> 0 us
  Pallas kernels: 35.7 us -> 37.1 us
    unnamed x13 -> x0, local copies, waits for them, and re-layouts: 7.32 us -> none
    pallas_call x1 -> x2, Pallas kernels: 35.7 us -> 37.1 us  [the longest x1 35.2 us: per_device(): pl.pallas_call(functools.partial(kernel, n), out_shape=(pltpu.VMEM((cols,...]
where the time goes in v2:
time: 38 us; the launch traced here: 37.7 us
  Pallas kernels  37.1 us (98%)
  between operations  0.64 us (2%)
    pallas_call x1, Pallas kernels, per_device(): pl.pallas_call(functools.partial(kernel, n), out_shape=(pltpu.VMEM((cols,...  35.2 us
    pallas_call x1, Pallas kernels, per_device(): pl.pallas_call(finish, out_shape=(jax.ShapeDtypeStruct((cols, scen), F32)...  1.84 us

profile of v2, /device:TPU:0, one launch (start us, length us, event | category | flops | bytes accessed | tf_op | source)
XLA Modules:
  0.0 37.7 jit_solution(8176837263198421895)
XLA Ops:
  0.6 35.2 %shard_map.85 = (f32[3072,128]{1,0:T(8,128)S(1)}, f32[1024,128]{1,0:T(8,128)S(1)}, f32[8,128]{1,0:T(8,128)S(1)}) custom-call(bf16[8,32,128,128]{3,2,1,0:T(8,128)(2,1)} %tiles_hbm.1, s32[8,32]{1,0:T(8,128)} %ids_ref.1, f32[24,128]{1,0:T(8,128)} %bitcast.2, f32[1024,128]{1,0:T(8,128)} %rhs_hbm.1, f32[3072,128]{1,0:T(8,128)} %primal_hbm.1, f32[1024,128]{1,0:T(8,128)} %dual_hbm.1), custom_call_target="tpu_custom_call" | custom-call | flops 4026531840 | bytes 11534336 | tf_op jit(solution)/shard_map/pallas_call | solution.py:390
  35.9 1.8 %shard_map.86 = (f32[3072,128]{1,0:T(8,128)}, f32[1024,128]{1,0:T(8,128)}, f32[1,128]{1,0:T(1,128)}) custom-call(f32[3072,128]{1,0:T(8,128)S(1)} %get-tuple-element.9.primal_in, f32[1024,128]{1,0:T(8,128)S(1)} %get-tuple-element.10.dual_in, f32[8,128]{1,0:T(8,128)S(1)} %get-tuple-element.11.totals), custom_call_target="tpu_custom_call" | custom-call | tf_op jit(solution)/shard_map/pallas_call | solution.py:414

commit v3 on v2

--- a/solution.py
+++ b/solution.py
@@ -77,14 +77,6 @@
 
     barrier = pltpu.get_barrier_semaphore()
 
-    def greet(k, carry):
-        pl.semaphore_signal(
-            barrier, inc=1, device_id={"band": lax.rem(me + k, n)}, device_id_type=MESH
-        )
-        return carry
-
-    lax.fori_loop(1, n, greet, None)
-
     def load_rows(start, size, k):
         return pltpu.make_async_copy(
             primal_hbm.at[pl.ds(start, size)], primal.at[pl.ds(start, size)], in_sem.at[k]
@@ -103,6 +95,10 @@
     ]
     head.start()
     tail.start()
+    for k in [1, n - 1] + list(range(2, n - 1)):
+        pl.semaphore_signal(
+            barrier, inc=1, device_id={"band": lax.rem(me + k, n)}, device_id_type=MESH
+        )
     rhs_in.start()
     for copy in tile_in[:2]:
         copy.start()
@@ -110,16 +106,6 @@
     for copy in tile_in[2:]:
         copy.start()
     dual_in.start()
-
-    base = me * col_blocks - MB
-    local = lax.rem(ids_ref[...] - base + total_blocks, total_blocks)
-    lane = lax.broadcasted_iota(jnp.int32, (row_blocks, BLK), 1)
-    inverse = jnp.full((row_blocks, BLK), tile_count, jnp.int32)
-    for t in range(tile_count):
-        inverse = jnp.where(lane == local[:, t : t + 1], t, inverse)
-    inv_v[...] = inverse
-    inv_copy = pltpu.make_async_copy(inv_v, inv_s, inv_sem)
-    inv_copy.start()
 
     def chunk(ref, c):
         return ref.at[pl.ds(c * PAIR, PAIR)]
@@ -150,43 +136,28 @@
         to_left[c].start()
         to_right[c].start()
 
-    def share(buf, send_sems, recv_sems, k):
-        peer = lax.rem(me + k, n)
+    def share(buf, send_sems, recv_sems, k, slot, peer):
         return pltpu.make_async_remote_copy(
-            src_ref=buf.at[me],
-            dst_ref=buf.at[me],
-            send_sem=send_sems.at[peer],
-            recv_sem=recv_sems.at[me],
+            src_ref=buf.at[slot],
+            dst_ref=buf.at[slot],
+            send_sem=send_sems.at[k],
+            recv_sem=recv_sems.at[k],
             device_id={"band": peer},
             device_id_type=MESH,
         )
 
-    def collect(buf, send_sems, recv_sems, k):
-        peer = lax.rem(me + k, n)
-        return pltpu.make_async_remote_copy(
-            src_ref=buf.at[peer],
-            dst_ref=buf.at[peer],
-            send_sem=send_sems.at[peer],
-            recv_sem=recv_sems.at[peer],
-            device_id={"band": peer},
-            device_id_type=MESH,
-        )
-
     def share_all(buf, send_sems, recv_sems):
-        def step(k, carry):
-            share(buf, send_sems, recv_sems, k).start()
-            return carry
-
-        lax.fori_loop(1, n, step, None)
+        copies = [
+            share(buf, send_sems, recv_sems, k, me, lax.rem(me + k, n)) for k in range(1, n)
+        ]
+        for copy in copies:
+            copy.start()
+        return copies
 
     def collect_all(buf, send_sems, recv_sems):
-        def step(k, carry):
-            copy = collect(buf, send_sems, recv_sems, k)
-            copy.wait_recv()
-            copy.wait_send()
-            return carry
-
-        lax.fori_loop(1, n, step, None)
+        for k in range(1, n):
+            source = lax.rem(me + n - k, n)
+            share(buf, send_sems, recv_sems, k, source, lax.rem(me + k, n)).wait_recv()
         return jnp.sum(buf[...], axis=0)
 
     def stack(first, second):
@@ -196,7 +167,17 @@
     rhs_sq = jnp.sum(rhs[...] * rhs[...], axis=0, keepdims=True)
     cost_sq = jnp.sum(cost_ref[...] * cost_ref[...], axis=0, keepdims=True)
     norm_buf[me] = stack(rhs_sq, cost_sq)
-    share_all(norm_buf, norm_send, norm_recv)
+    norm_copies = share_all(norm_buf, norm_send, norm_recv)
+
+    base = me * col_blocks - MB
+    local = lax.rem(ids_ref[...] - base + total_blocks, total_blocks)
+    lane = lax.broadcasted_iota(jnp.int32, (row_blocks, BLK), 1)
+    inverse = jnp.full((row_blocks, BLK), tile_count, jnp.int32)
+    for t in range(tile_count):
+        inverse = jnp.where(lane == local[:, t : t + 1], t, inverse)
+    inv_v[...] = inverse
+    inv_copy = pltpu.make_async_copy(inv_v, inv_s, inv_sem)
+    inv_copy.start()
 
     for w in range(col_blocks):
         cost_col[w * BLK : (w + 1) * BLK] = jnp.transpose(
@@ -321,24 +302,33 @@
     dual_out[...] = dual_next
     dual_obj = jnp.sum(rhs[...] * dual_next, axis=0, keepdims=True)
     obj_buf[me] = stack(primal_obj, dual_obj)
-    share_all(obj_buf, obj_send, obj_recv)
-    for copy in to_left + to_right + terms_left + terms_right + flow_left + flow_right:
+    obj_copies = share_all(obj_buf, obj_send, obj_recv)
+    for copy in norm_copies + to_left + to_right + terms_left + terms_right + flow_left + flow_right:
         copy.wait_send()
     totals_out[...] = collect_all(obj_buf, obj_send, obj_recv)
+    for copy in obj_copies:
+        copy.wait_send()
 
 
 def finish(primal_in, dual_in, totals, primal_out, dual_out, gap_out, sems):
-    first = pltpu.make_async_copy(primal_in, primal_out, sems.at[0])
-    second = pltpu.make_async_copy(dual_in, dual_out, sems.at[1])
-    first.start()
-    second.start()
+    parts = sems.shape[0] // 2
+    copies = []
+    for k in range(parts):
+        for j, (source, target) in enumerate(((primal_in, primal_out), (dual_in, dual_out))):
+            size = source.shape[0] // parts
+            at = pl.ds(k * size, size)
+            copies.append(
+                pltpu.make_async_copy(source.at[at], target.at[at], sems.at[2 * k + j])
+            )
+    for copy in copies:
+        copy.start()
     primal_total = totals[0:1]
     dual_total = totals[1:2]
     gap_out[...] = (primal_total - dual_total) / (
         1.0 + jnp.abs(primal_total) + jnp.abs(dual_total)
     )
-    first.wait()
-    second.wait()
+    for copy in copies:
+        copy.wait()
 
 
 def per_device(n, tile_blocks, column_ids, arc_cost, demand_rhs, primal_start, dual_start):
@@ -420,7 +410,7 @@
         ),
         in_specs=[any_space, any_space, vmem],
         out_specs=(hbm, hbm, vmem),
-        scratch_shapes=[dma((2,))],
+        scratch_shapes=[dma((8,))],
         compiler_params=pltpu.CompilerParams(vmem_limit_bytes=1024 * 1024),
     )(*outs)
     return primal_next, dual_next, gap.reshape(scen)

time: 38 us -> 37.4 us (0.984)
  Pallas kernels: 37.1 us -> 36.5 us
    pallas_call x1, Pallas kernels: 35.2 us -> 34.6 us  [per_device(): pl.pallas_call(functools.partial(kernel, n), out_shape=(pltpu.VMEM((cols,...]
where the time goes in v3:
time: 37.4 us; the launch traced here: 37.1 us
  Pallas kernels  36.5 us (98%)
  between operations  0.64 us (2%)
    pallas_call x1, Pallas kernels, per_device(): pl.pallas_call(functools.partial(kernel, n), out_shape=(pltpu.VMEM((cols,...  34.6 us
    pallas_call x1, Pallas kernels, per_device(): pl.pallas_call(finish, out_shape=(jax.ShapeDtypeStruct((cols, scen), F32)...  1.88 us

profile of v3, /device:TPU:0, one launch (start us, length us, event | category | flops | bytes accessed | tf_op | source)
XLA Modules:
  0.0 37.1 jit_solution(12647760163854800740)
XLA Ops:
  0.6 34.6 %shard_map.85 = (f32[3072,128]{1,0:T(8,128)S(1)}, f32[1024,128]{1,0:T(8,128)S(1)}, f32[8,128]{1,0:T(8,128)S(1)}) custom-call(bf16[8,32,128,128]{3,2,1,0:T(8,128)(2,1)} %tiles_hbm.1, s32[8,32]{1,0:T(8,128)} %ids_ref.1, f32[24,128]{1,0:T(8,128)} %bitcast.2, f32[1024,128]{1,0:T(8,128)} %rhs_hbm.1, f32[3072,128]{1,0:T(8,128)} %primal_hbm.1, f32[1024,128]{1,0:T(8,128)} %dual_hbm.1), custom_call_target="tpu_custom_call" | custom-call | flops 4026531840 | bytes 11534336 | tf_op jit(solution)/shard_map/pallas_call | solution.py:380
  35.2 1.9 %shard_map.86 = (f32[3072,128]{1,0:T(8,128)}, f32[1024,128]{1,0:T(8,128)}, f32[1,128]{1,0:T(1,128)}) custom-call(f32[3072,128]{1,0:T(8,128)S(1)} %get-tuple-element.9.primal_in, f32[1024,128]{1,0:T(8,128)S(1)} %get-tuple-element.10.dual_in, f32[8,128]{1,0:T(8,128)S(1)} %get-tuple-element.11.totals), custom_call_target="tpu_custom_call" | custom-call | tf_op jit(solution)/shard_map/pallas_call | solution.py:404
